TPU v7x, 512 devices: a whole 4x4x16 slice. The times are simulated.
512 devices in a mesh: lat: 32 (over x, y, core), lon: 16 (over z).
Axes of the slice: x: 4, y: 4, z: 16, core: 2. Of those that a mesh axis runs over, the one named last changes fastest.
Arguments:
- grid_in: bfloat16 [384, 768, 384], P('lat', 'lon'), may hold values from -6 to 6
- grid_cot: bfloat16 [384, 768, 384], P('lat', 'lon'), may hold values from -6 to 6
- legendre: bfloat16 [384, 384, 384], P('lat'), as said below
- filters: float32 [384, 2, 384], P(None, None, 'lon'), may hold values from -6 to 6
Outputs:
- grad_grid: bfloat16 [384, 768, 384], P('lat', 'lon')
- grad_filters: float32 [384, 2, 384], P('lat', None, 'lon')
Inputs may be any that keep to these rules, and one draw needn't show every extreme that they name: legendre[m, q, l] is zero wherever the degree l is below the order m.
All inputs are finite; a program needn't handle non-finite values.
Results may differ from a plain program's by a relative error of at most 0.008.
Values may be sent and summed in bfloat16 or wider, within the bound.
A program may use at most 64 MiB of HBM per device.

v0:
```python
import math

import jax
import jax.numpy as jnp
from jax import lax
from jax.sharding import PartitionSpec as P


def fourier_table(points, degrees):
    points_at = lax.broadcasted_iota(jnp.int32, (points, degrees), 0)
    wave_num = lax.broadcasted_iota(jnp.int32, (points, degrees), 1)
    phases = points_at * wave_num % points
    angles = phases.astype(jnp.float32) * (2.0 * math.pi / points)
    fourier = jnp.stack([jnp.cos(angles), -jnp.sin(angles)], axis=2) * points ** (-0.5)
    return fourier.reshape(points, 2 * degrees).astype(jnp.bfloat16)


def degree_spans(degrees):
    span_size = 128
    return [(first_deg, span_size) for first_deg in range(0, degrees, span_size)]


def analyse(legendre, spectra):
    orders_dev, lat_rows, degrees = legendre.shape
    chan_count = spectra.shape[1]
    shaped = spectra.reshape(lat_rows, chan_count, orders_dev, 2)
    pieces = []
    for first_deg, span_size in degree_spans(degrees):
        part_table = legendre[:, :, first_deg : first_deg + span_size]

        def analyse_compute(part_table=part_table):
            return jnp.einsum(
                "oql,qcor->olrc", part_table, shaped, preferred_element_type=jnp.float32
            )

        pieces.append(analyse_compute())
    return jnp.concatenate(pieces, axis=1)


def synthesise(legendre, back):
    orders_dev, lat_rows, degrees = legendre.shape
    chan_count = back.shape[3]
    total = jnp.zeros((lat_rows, chan_count, orders_dev, 2), jnp.float32)
    for first_deg, span_size in degree_spans(degrees):
        part_table = legendre[:, :, first_deg : first_deg + span_size]
        part_back = back[:, first_deg : first_deg + span_size]

        def synthesise_compute(part_table=part_table, part_back=part_back):
            return jnp.einsum(
                "oql,olrc->qcor", part_table, part_back, preferred_element_type=jnp.float32
            )

        total = total + synthesise_compute()
    return total


def local(grid_in, grid_cot, legendre, filters):
    lat_dev, lon_dev, channels = grid_in.shape
    longitudes = lon_dev * lax.axis_size("lon")
    orders_dev, lat_rows, degrees = legendre.shape
    fourier = fourier_table(longitudes, degrees)
    lon_in, lon_cot = (
        lax.all_to_all(grid_in, "lon", split_axis=2, concat_axis=1, tiled=True),
        lax.all_to_all(grid_cot, "lon", split_axis=2, concat_axis=1, tiled=True),
    )
    spec_in = jnp.einsum("qnc,nk->qck", lon_in, fourier, preferred_element_type=jnp.float32).astype(
        jnp.bfloat16
    )
    spec_cot = jnp.einsum(
        "qnc,nk->qck", lon_cot, fourier, preferred_element_type=jnp.float32
    ).astype(jnp.bfloat16)
    coeff_in = analyse(
        legendre, lax.all_to_all(spec_in, "lat", split_axis=2, concat_axis=0, tiled=True)
    )
    coeff_cot = analyse(
        legendre, lax.all_to_all(spec_cot, "lat", split_axis=2, concat_axis=0, tiled=True)
    )
    in_re, in_im = (coeff_in[:, :, 0, :], coeff_in[:, :, 1, :])
    cot_re, cot_im = (coeff_cot[:, :, 0, :], coeff_cot[:, :, 1, :])
    local_grad = jnp.stack(
        [
            jnp.sum(in_re * cot_re + in_im * cot_im, axis=0),
            jnp.sum(in_re * cot_im - in_im * cot_re, axis=0),
        ],
        axis=1,
    )
    grad_filters = lax.psum_scatter(local_grad, "lat", scatter_dimension=0, tiled=True)
    gain_re, gain_im = (filters[:, 0, :], filters[:, 1, :])
    back = jnp.stack(
        [gain_re * cot_re + gain_im * cot_im, gain_re * cot_im - gain_im * cot_re], axis=2
    ).astype(jnp.bfloat16)
    order_spec = synthesise(legendre, back)
    order_spec = order_spec.astype(jnp.bfloat16).reshape(lat_rows, back.shape[3], 2 * orders_dev)
    spec_back = lax.all_to_all(order_spec, "lat", split_axis=0, concat_axis=2, tiled=True)
    grid_back = jnp.einsum(
        "qck,nk->qnc", spec_back, fourier, preferred_element_type=jnp.float32
    ).astype(jnp.bfloat16)
    grad_grid = lax.all_to_all(grid_back, "lon", split_axis=1, concat_axis=2, tiled=True)
    return (grad_grid, grad_filters)


def solution(mesh):
    return jax.shard_map(
        local,
        mesh=mesh,
        in_specs=(
            P("lat", "lon", None),
            P("lat", "lon", None),
            P("lat", None, None),
            P(None, None, "lon"),
        ),
        out_specs=(P("lat", "lon", None), P("lat", None, "lon")),
        check_vma=False,
    )
```

profile of v0, /device:TPU:1, one launch (start us, length us, event | category | flops | bytes accessed | tf_op | source)
XLA Modules:
  0.0 366.8 jit_solution(9083882465901208937)
XLA Ops:
  9.3 2.6 reshape.98
  11.9 15.7 %all-to-all-start = ((bf16[16,2,6912]{2,1,0:T(2,128)(2,1)}), bf16[16,2,6912]{2,1,0:T(2,128)(2,1)S(1)}, u32[]{:S(2)}, u32[]{:S(2)}) async-start(bf16[16,2,6912]{2,1,0:T(2,128)(2,1)} %reshape.98), calls=%async_computation | async-start | bytes 884736 | tf_op jit(solution)/shard_map/all_to_all | solution.py:64
  29.2 2.6 reshape.106
  31.8 16.3 %all-to-all-done = bf16[16,2,6912]{2,1,0:T(2,128)(2,1)S(1)} async-done(((bf16[16,2,6912]{2,1,0:T(2,128)(2,1)}), bf16[16,2,6912]{2,1,0:T(2,128)(2,1)S(1)}, u32[]{:S(2)}, u32[]{:S(2)}) %all-to-all-start) | async-done | bytes 442400 | tf_op jit(solution)/shard_map/all_to_all | solution.py:64
  48.1 11.6 %all-to-all-start.4 = ((bf16[16,2,6912]{2,1,0:T(2,128)(2,1)}), bf16[16,2,6912]{2,1,0:T(2,128)(2,1)}, u32[]{:S(2)}, u32[]{:S(2)}) async-start(bf16[16,2,6912]{2,1,0:T(2,128)(2,1)} %reshape.106), calls=%async_computation.4 | async-start | bytes 884736 | tf_op jit(solution)/shard_map/all_to_all | solution.py:63
  59.7 4.8 %sine_negate_fusion = (f32[768,384,1]{1,0,2:T(8,128)S(1)}, f32[768,384,1]{1,0,2:T(8,128)S(1)}) fusion(), kind=kLoop, calls=%fused_computation.27 | loop fusion | flops 2949120 | bytes 2359296 | tf_op jit(solution)/shard_map/neg | solution.py:14
  71.5 2.3 all_to_all.77
  75.2 3.8 %copy.63 = bf16[12,24,768]{1,0,2:T(8,128)(2,1)S(1)} copy(bf16[12,24,768]{2,1,0:T(8,128)(2,1)} %convert_bitcast_fusion.1) | data formatting | bytes 884736 | tf_op jit(solution)/shard_map/convert_element_type | solution.py:71
  79.0 4.3 %reshape.100 = bf16[32,2,3456]{2,1,0:T(2,128)(2,1)} reshape(bf16[768,12,24]{2,1,0:T(8,128)(2,1)S(1)} %bitcast.134) | data formatting | bytes 884736
  83.4 10.0 %all-to-all-start.1 = ((bf16[32,2,3456]{2,1,0:T(2,128)(2,1)}), bf16[32,2,3456]{2,1,0:T(2,128)(2,1)}, u32[]{:S(2)}, u32[]{:S(2)}) async-start(bf16[32,2,3456]{2,1,0:T(2,128)(2,1)} %reshape.100), calls=%async_computation.1 | async-start | bytes 884736 | tf_op jit(solution)/shard_map/all_to_all | solution.py:76
  93.4 3.3 reshape.107
  100.1 3.8 %copy.78 = bf16[12,24,768]{1,0,2:T(8,128)(2,1)S(1)} copy(bf16[12,24,768]{2,1,0:T(8,128)(2,1)} %convert_bitcast_fusion) | data formatting | bytes 884736 | tf_op jit(solution)/shard_map/convert_element_type | solution.py:66
  103.9 3.8 %reshape.108 = bf16[32,2,3456]{2,1,0:T(2,128)(2,1)} reshape(bf16[768,12,24]{2,1,0:T(8,128)(2,1)S(1)} %bitcast.135) | data formatting | bytes 884736
  107.7 7.8 %all-to-all-start.5 = ((bf16[32,2,3456]{2,1,0:T(2,128)(2,1)}), bf16[32,2,3456]{2,1,0:T(2,128)(2,1)}, u32[]{:S(2)}, u32[]{:S(2)}) async-start(bf16[32,2,3456]{2,1,0:T(2,128)(2,1)} %reshape.108), calls=%async_computation.5 | async-start | bytes 884736 | tf_op jit(solution)/shard_map/all_to_all | solution.py:73
  115.5 5.6 %reshape.101 = bf16[768,12,24]{2,1,0:T(8,128)(2,1)} reshape(bf16[32,2,3456]{2,1,0:T(2,128)(2,1)} %all-to-all-done.1) | data formatting | bytes 884736
  121.2 4.1 %copy.65 = bf16[32,12,24,24]{2,3,1,0:T(8,128)(2,1)} copy(bf16[32,12,24,24]{2,1,3,0:T(8,128)(2,1)} %bitcast.138) | data formatting | bytes 884736 | tf_op jit(solution)/shard_map/all_to_all | solution.py:76
  125.3 6.4 %copy.66 = bf16[384,24,12,2]{0,1,3,2:T(8,128)(2,1)} copy(bf16[384,24,12,2]{1,3,2,0:T(2,128)(2,1)} %bitcast.141) | data formatting | bytes 884736 | tf_op jit(solution)/shard_map/reshape | solution.py:26
  136.0 5.6 %reshape.109 = bf16[768,12,24]{2,1,0:T(8,128)(2,1)} reshape(bf16[32,2,3456]{2,1,0:T(2,128)(2,1)} %all-to-all-done.5) | data formatting | bytes 884736
  141.6 3.9 %copy.80 = bf16[32,12,24,24]{2,3,1,0:T(8,128)(2,1)} copy(bf16[32,12,24,24]{2,1,3,0:T(8,128)(2,1)} %bitcast.139) | data formatting | bytes 884736 | tf_op jit(solution)/shard_map/all_to_all | solution.py:73
  145.6 6.3 %copy.81 = bf16[384,24,12,2]{0,1,3,2:T(8,128)(2,1)} copy(bf16[384,24,12,2]{1,3,2,0:T(2,128)(2,1)} %bitcast.142) | data formatting | bytes 884736 | tf_op jit(solution)/shard_map/reshape | solution.py:26
  159.8 3.0 copy.69
  162.8 3.1 reshape.102
  165.9 18.2 %all_to_all.102 = bf16[32,2,3456]{2,1,0:T(2,128)(2,1)S(1)} all-to-all(bf16[32,2,3456]{2,1,0:T(2,128)(2,1)S(1)} %reshape.102), channel_id=1, replica_groups=mesh['lat'=32,'lon'=16] {'lat'}, dimensions={0} | all-to-all | bytes 884736 | tf_op jit(solution)/shard_map/all_to_all | solution.py:94
  184.1 3.3 reshape.103
  187.4 2.4 copy.70
  189.7 4.3 %all_to_all.84 = bf16[12,24,768]{2,1,0:T(8,128)(2,1)S(1)} reshape(bf16[12,24,32,24]{3,2,1,0:T(8,128)(2,1)} %copy.70) | data formatting | bytes 884736 | tf_op jit(solution)/shard_map/all_to_all | solution.py:94
  195.3 3.8 %copy.72 = bf16[12,768,24]{2,0,1:T(8,128)(2,1)S(1)} copy(bf16[12,768,24]{1,2,0:T(8,128)(2,1)} %fusion.2) | data formatting | bytes 884736 | tf_op jit(solution)/shard_map/convert_element_type | solution.py:97
  199.2 3.8 %reshape.104 = bf16[16,2,6912]{2,1,0:T(2,128)(2,1)} reshape(bf16[768,12,24]{2,1,0:T(8,128)(2,1)S(1)} %bitcast.136) | data formatting | bytes 884736
  202.9 10.2 %all-to-all-start.3 = ((bf16[16,2,6912]{2,1,0:T(2,128)(2,1)}), bf16[16,2,6912]{2,1,0:T(2,128)(2,1)}, u32[]{:S(2)}, u32[]{:S(2)}) async-start(bf16[16,2,6912]{2,1,0:T(2,128)(2,1)} %reshape.104), calls=%async_computation.3 | async-start | bytes 884736 | tf_op jit(solution)/shard_map/all_to_all | solution.py:98
  216.1 131.8 %all-reduce.3.cloned.1.call-done = f32[384,2,24]{2,1,0:T(2,128)} async-done(((f32[384,2,24]{2,1,0:T(2,128)}), f32[384,2,24]{2,1,0:T(2,128)}) %all-reduce.3.cloned.1.call-update) | async-done | bytes 73744
  349.2 4.7 %reshape.105 = bf16[768,12,24]{2,1,0:T(8,128)(2,1)S(1)} reshape(bf16[16,2,6912]{2,1,0:T(2,128)(2,1)} %all-to-all-done.3) | data formatting | bytes 884736
  353.9 3.6 copy.73
  (68 shorter events, 34.7 us)
Async XLA Ops:
  9.3 18.3 %copy-start.9 = (bf16[12,48,384]{2,1,0:T(8,128)(2,1)S(1)}, bf16[12,48,384]{2,1,0:T(8,128)(2,1)}, u32[]{:S(2)}) copy-start(bf16[12,48,384]{2,1,0:T(8,128)(2,1)} %param.4) | copy-start | bytes 1327108
  11.9 36.2 %all-to-all-start = ((bf16[16,2,6912]{2,1,0:T(2,128)(2,1)}), bf16[16,2,6912]{2,1,0:T(2,128)(2,1)S(1)}, u32[]{:S(2)}, u32[]{:S(2)}) async-start(bf16[16,2,6912]{2,1,0:T(2,128)(2,1)} %reshape.98), calls=%async_computation | async-start | bytes 884736 | tf_op jit(solution)/shard_map/all_to_all | solution.py:64
  48.1 35.3 %all-to-all-start.4 = ((bf16[16,2,6912]{2,1,0:T(2,128)(2,1)}), bf16[16,2,6912]{2,1,0:T(2,128)(2,1)}, u32[]{:S(2)}, u32[]{:S(2)}) async-start(bf16[16,2,6912]{2,1,0:T(2,128)(2,1)} %reshape.106), calls=%async_computation.4 | async-start | bytes 884736 | tf_op jit(solution)/shard_map/all_to_all | solution.py:63
  66.2 0.9 copy-start.14
  67.1 6.8 %copy-start.1 = (bf16[768,768]{0,1:T(8,128)(2,1)}, bf16[768,768]{0,1:T(8,128)(2,1)S(1)}, u32[]{:S(2)}) copy-start(bf16[768,768]{0,1:T(8,128)(2,1)S(1)} %convert_element_type.63) | copy-start | bytes 3538948
  83.4 24.4 %all-to-all-start.1 = ((bf16[32,2,3456]{2,1,0:T(2,128)(2,1)}), bf16[32,2,3456]{2,1,0:T(2,128)(2,1)}, u32[]{:S(2)}, u32[]{:S(2)}) async-start(bf16[32,2,3456]{2,1,0:T(2,128)(2,1)} %reshape.100), calls=%async_computation.1 | async-start | bytes 884736 | tf_op jit(solution)/shard_map/all_to_all | solution.py:76
  97.4 1.4 copy-start.2
  107.7 28.2 %all-to-all-start.5 = ((bf16[32,2,3456]{2,1,0:T(2,128)(2,1)}), bf16[32,2,3456]{2,1,0:T(2,128)(2,1)}, u32[]{:S(2)}, u32[]{:S(2)}) async-start(bf16[32,2,3456]{2,1,0:T(2,128)(2,1)} %reshape.108), calls=%async_computation.5 | async-start | bytes 884736 | tf_op jit(solution)/shard_map/all_to_all | solution.py:73
  121.2 10.5 %copy-start = (bf16[12,384,384]{2,1,0:T(8,128)(2,1)S(1)}, bf16[12,384,384]{2,1,0:T(8,128)(2,1)}, u32[]{:S(2)}) copy-start(bf16[12,384,384]{2,1,0:T(8,128)(2,1)} %param.6) | copy-start | bytes 10616836
  131.6 2.2 copy-start.4
  151.9 1.5 copy-start.5
  153.8 1.0 copy-start.6
  153.8 1.0 copy-start.7
  153.8 1.1 copy-start.8
  155.0 0.8 copy-start.10
  155.0 0.8 copy-start.11
  189.7 4.3 %copy-start.3 = (bf16[768,768]{0,1:T(8,128)(2,1)S(1)}, bf16[768,768]{0,1:T(8,128)(2,1)}, u32[]{:S(2)}) copy-start(bf16[768,768]{0,1:T(8,128)(2,1)} %copy-done.1) | copy-start | bytes 3538948
  199.2 14.0 %copy-start.12 = (f32[384,24]{0,1:T(8,128)S(1)}, f32[384,24]{0,1:T(8,128)}, u32[]{:S(2)}) copy-start(f32[384,24]{0,1:T(8,128)} %get-tuple-element.8) | copy-start | bytes 110596
  199.2 14.0 %copy-start.13 = (f32[384,24]{0,1:T(8,128)S(1)}, f32[384,24]{0,1:T(8,128)}, u32[]{:S(2)}) copy-start(f32[384,24]{0,1:T(8,128)} %get-tuple-element.9) | copy-start | bytes 110596
  202.9 146.2 %all-to-all-start.3 = ((bf16[16,2,6912]{2,1,0:T(2,128)(2,1)}), bf16[16,2,6912]{2,1,0:T(2,128)(2,1)}, u32[]{:S(2)}, u32[]{:S(2)}) async-start(bf16[16,2,6912]{2,1,0:T(2,128)(2,1)} %reshape.104), calls=%async_computation.3 | async-start | bytes 884736 | tf_op jit(solution)/shard_map/all_to_all | solution.py:98
  213.1 134.8 %all-reduce.3.cloned.1.call-start = ((), (), s32[]{:S(2)}) async-start(), calls=%async_computation.6 | async-start | bytes 786432
Sparse Core Ops, SparseCore 0:
  217.2 130.6 all-reduce.2
where the time goes:
time: 372 us; the launch traced here: 367 us
  waiting for transfers between devices  148 us (40%)
  local copies, waits for them, and re-layouts  110 us (30%)
  starting transfers between devices  55.4 us (15%)
  blocking collectives  18.2 us (5%)
  between operations  15.3 us (4%)
  matrix products  12 us (3%)
  other arithmetic  7.63 us (2%)
    unnamed x2, waiting for transfers between devices  132 us
    unnamed x47, local copies, waits for them, and re-layouts  55 us
    all_to_all x1, blocking collectives, local(): lax.all_to_all(order_spec, 'lat', split_axis=0, concat_axis=2, tiled=True)  18.2 us
    all_to_all x1, waiting for transfers between devices, local(): lax.all_to_all(grid_cot, 'lon', split_axis=2, concat_axis=1, tiled=True)  16.3 us
    all_to_all x1, starting transfers between devices, local(): lax.all_to_all(grid_cot, 'lon', split_axis=2, concat_axis=1, tiled=True)  15.7 us
    reshape x2, local copies, waits for them, and re-layouts, analyse(): shaped = spectra.reshape(lat_rows, chan_count, orders_dev, 2)  12.7 us
    all_to_all x1, starting transfers between devices, local(): lax.all_to_all(grid_in, 'lon', split_axis=2, concat_axis=1, tiled=True)  11.6 us
    all_to_all x1, starting transfers between devices, local(): lax.all_to_all(grid_back, 'lon', split_axis=1, concat_axis=2, tiled=True)  10.2 us
  transfers between devices with their start and end apart: 6, of which 2 were waited for; matrix products, arithmetic and copies ran while one was open for 17% of the time, Pallas kernels for 0%

commit v1 on v0

v1 whole, which is shorter than its diff:
```python
import math

import jax
import jax.numpy as jnp
import ml_dtypes
import numpy as np
from jax import lax
from jax.experimental import pallas as pl
from jax.experimental.pallas import tpu as pltpu
from jax.sharding import PartitionSpec as P

MESH = pl.DeviceIdType.MESH
BF16 = jnp.bfloat16
F32 = jnp.float32

NZ, NL = 16, 32
LATS, LONS, DEGREES, CHANNELS = 384, 768, 384, 384
Q, N, C = LATS // NL, LONS // NZ, CHANNELS // NZ
M = DEGREES // NL
RING = 384
GROUPS = N // 16

PARTS = ((0, 7), (7, 5))
WIDTH = tuple(C * rows for _, rows in PARTS)
TILES = tuple(-(-GROUPS * w // 128) for w in WIDTH)


def fourier_tables():
    points = np.arange(LONS, dtype=np.int64)[:, None]
    order = np.arange(DEGREES, dtype=np.int64)[None, :]
    phases = (points * order) % LONS
    angles = phases.astype(np.float32) * np.float32(2.0 * math.pi / LONS)
    pair = np.stack([np.cos(angles), -np.sin(angles)], axis=2) * np.float32(LONS ** (-0.5))
    table = pair.reshape(LONS, 2 * DEGREES).astype(ml_dtypes.bfloat16)
    n_of = np.arange(LONS).reshape(NZ, GROUPS, 16).transpose(1, 0, 2).reshape(-1)
    k = np.arange(2 * DEGREES).reshape(NL, 2 * M)
    k_of = np.concatenate([k[:, :16].reshape(-1), k[:, 16:].reshape(-1)])
    back = table[n_of][:, k_of]
    return np.ascontiguousarray(back.T), np.ascontiguousarray(back)


def lanes(rows):
    return lax.broadcasted_iota(jnp.int32, (rows, 128), 1)


def merge_blocks(rows, pick):
    at = lanes(rows)
    tiles = []
    for t in range(3):
        value = None
        for b in range(16):
            low, high = C * b - 128 * t, C * (b + 1) - 128 * t
            if high <= 0 or low >= 128:
                continue
            block = pick(b, t)
            value = block if value is None else jnp.where(at >= low, block, value)
        tiles.append(value)
    return jnp.concatenate(tiles, axis=1)


def block_transpose(rows, count, load, store):
    zero = jnp.zeros((rows, 128), F32)
    for x in range(count):
        ring = merge_blocks(
            rows, lambda b, t: load((b - x) % 16, t) if (b - x) % 16 < count else zero
        )
        store(x, pltpu.roll(ring, (-C * x) % RING, 1) if x else ring)


def one_hot(size, column_of):
    row = lax.broadcasted_iota(jnp.int32, (size, size), 0)
    column = lax.broadcasted_iota(jnp.int32, (size, size), 1)
    return jnp.where(column == column_of(row), 1.0, 0.0).astype(BF16)


def dot(a, b):
    return jnp.dot(a, b, preferred_element_type=F32)


def kernel(
    in_hbm, cot_hbm, leg_hbm, filt_hbm, fwd_hbm, bwd_hbm,
    grad_out, filt_out,
    grid, leg, legp, filt, fwd, bwd, perm, permt, ring, xbuf, dbuf, strans, sback, coef, acc, gsum,
    zs_a, zs_b, zr_a, zr_b, ls_a, ls_b, lr_a, lr_b, gs, gr,
    load_sem, own_sem, zss, zrs, lss, lrs, gss, grs,
):
    lat, lon = lax.axis_index("lat"), lax.axis_index("lon")
    zs, zr, ls, lr = (zs_a, zs_b), (zr_a, zr_b), (ls_a, ls_b), (lr_a, lr_b)

    loads = [
        pltpu.make_async_copy(cot_hbm, grid.at[0], load_sem.at[0]),
        pltpu.make_async_copy(in_hbm, grid.at[1], load_sem.at[1]),
        pltpu.make_async_copy(leg_hbm, leg, load_sem.at[2]),
        pltpu.make_async_copy(fwd_hbm, fwd, load_sem.at[3]),
        pltpu.make_async_copy(bwd_hbm, bwd, load_sem.at[4]),
        pltpu.make_async_copy(filt_hbm, filt, load_sem.at[5]),
    ]
    for load in loads:
        load.start()
    barrier = pltpu.get_barrier_semaphore()

    def greet_lon(d, carry):
        pl.semaphore_signal(
            barrier, inc=1, device_id=(lat, lax.rem(lon + d, NZ)), device_id_type=MESH
        )
        return carry

    def greet_lat(d, carry):
        pl.semaphore_signal(
            barrier, inc=1, device_id=(lax.rem(lat + d, NL), lon), device_id_type=MESH
        )
        return carry

    lax.fori_loop(1, NZ, greet_lon, 0)
    lax.fori_loop(1, NL, greet_lat, 0)

    def send_lon(phase, p):
        def step(s, carry):
            half = lax.div(s + 1, 2)
            d = jnp.where(lax.rem(s, 2) == 0, 8 + half, 8 - half)
            to = lax.rem(lon + d, NZ)
            pltpu.make_async_remote_copy(
                src_ref=zs[p].at[phase, to],
                dst_ref=zr[p].at[phase, lon],
                send_sem=zss.at[phase, p],
                recv_sem=zrs.at[phase, p],
                device_id=(lat, to),
                device_id_type=MESH,
            ).start()
            return carry

        lax.fori_loop(0, NZ - 1, step, 0)
        own = pltpu.make_async_copy(zs[p].at[phase, lon], zr[p].at[phase, lon], own_sem.at[0])
        own.start()
        own.wait()

    def wait_lon(phase, p, sem):
        some = zr[p].at[phase, pl.ds(0, NZ - 1)]
        pltpu.make_async_copy(some, some, sem.at[phase, p]).wait()

    def send_lat(phase, p):
        def step(s, carry):
            to = lax.rem(lat + NL - 1 - s, NL)
            pltpu.make_async_remote_copy(
                src_ref=ls[p].at[phase, to],
                dst_ref=lr[p].at[phase, lat],
                send_sem=lss.at[phase, p],
                recv_sem=lrs.at[phase, p],
                device_id=(to, lon),
                device_id_type=MESH,
            ).start()
            return carry

        lax.fori_loop(0, NL - 1, step, 0)
        own = pltpu.make_async_copy(ls[p].at[phase, lat], lr[p].at[phase, lat], own_sem.at[1])
        own.start()
        own.wait()

    def wait_lat(phase, p, sem):
        some = lr[p].at[phase, pl.ds(0, NL - 1)]
        pltpu.make_async_copy(some, some, sem.at[phase, p]).wait()

    def pack(a, p):
        first, rows = PARTS[p]
        for i in range(16):
            if i < rows:
                wide = grid[a, first + i].astype(F32)
                ring[i] = pltpu.roll(wide, C * i, 1) if i else wide
            else:
                ring[i] = jnp.zeros((N, RING), F32)

        def one(z, carry):
            merged = merge_blocks(
                N, lambda b, t: ring[lax.rem(b + NZ - z, NZ), :, 128 * t : 128 * (t + 1)]
            )
            tiles = [jnp.zeros((16, 128), F32) for _ in range(TILES[p])]
            for g in range(GROUPS):
                base, shift = divmod(WIDTH[p] * g, 128)
                moved = pltpu.roll(
                    merged[16 * g : 16 * (g + 1)], lax.rem(shift + RING - C * z + RING, RING), 1
                )
                tiles[base] = tiles[base] + moved[:, :128]
                if base + 1 < TILES[p]:
                    tiles[base + 1] = tiles[base + 1] + moved[:, 128:256]
            zs[p][a, z] = jnp.concatenate(tiles, axis=1).astype(BF16)
            return carry

        lax.fori_loop(0, NZ, one, 0)

    def analyse_lon(a, p):
        width = WIDTH[p]
        wait_lon(a, p, zrs)
        for g in range(GROUPS):
            base, shift = divmod(width * g, 128)
            window = zr[p][a, :, :, 128 * base : 128 * base + 256].reshape(256, 256)
            if shift:
                window = pltpu.roll(window.astype(F32), 256 - shift, 1).astype(BF16)
            xbuf[pl.ds(256 * g, 256), :] = window
        for r in range(3):
            dbuf[pl.ds(256 * r, 256), :] = dot(fwd[pl.ds(256 * r, 256), :], xbuf[...])
        low = dbuf[pl.ds(0, 512), :128].reshape(NL, 16, 128)
        ls[p][a, :, :, :128] = low.astype(BF16)
        high = dbuf[pl.ds(512, 256), :128].reshape(NL, 8, 128)
        tail = width - 128
        if tail > 0:
            at = lax.broadcasted_iota(jnp.int32, (512, 128), 1)
            first = jnp.where(at < tail, dbuf[pl.ds(0, 512), 128:], 0.0).reshape(NL, 16, 128)
            last = jnp.where(at[:256] < tail, dbuf[pl.ds(512, 256), 128:], 0.0)
            ends = first[:, :8] + (
                pltpu.roll(first[:, 8:].reshape(256, 128), tail, 1)
                + pltpu.roll(last, 2 * tail, 1)
            ).reshape(NL, 8, 128)
        else:
            ends = jnp.zeros((NL, 8, 128), F32)
        ls[p][a, :, :, 128:] = jnp.concatenate([high, ends], axis=1).astype(BF16)
        send_lat(a, p)

    def gather_orders(a):
        for p in range(2):
            wait_lat(a, p, lrs)
            flat = lr[p][a].reshape(512, 256)
            dbuf[pl.ds(0, 512), :] = dot(perm[...], flat)
            at = lanes(NL)
            tail = WIDTH[p] - 128
            start = C * PARTS[p][0]
            for kk in range(2 * M):
                i, t = (kk, 0) if kk < 16 else (kk - 16, 1)
                main = dbuf[pl.ds(NL * i, NL), 128 * t : 128 * (t + 1)]
                zero = jnp.zeros((NL, 128), F32)
                if tail > 0:
                    part = kk // 8
                    end = dbuf[pl.ds(NL * (8 + kk % 8), NL), 128:]
                    end = pltpu.roll(end, (-tail * part) % 128, 1) if part else end
                    end = jnp.where(at < tail, end, zero)
                else:
                    end = zero
                    main = jnp.where(at < WIDTH[p], main, zero)
                wide = jnp.concatenate([main, end, zero], axis=1)
                shift = (start + C * (kk % M)) % RING
                wide = pltpu.roll(wide, shift, 1) if shift else wide
                if p == 0:
                    ring[kk // M * M + kk % M, :NL] = wide
                else:
                    ring[kk, :NL] = ring[kk, :NL] + wide

    def analyse_lat(a):
        gather_orders(a)
        for h in range(2):
            def load(i, t, h=h):
                return ring[M * h + i, :NL, 128 * t : 128 * (t + 1)]

            def store(x, value):
                xform[pl.ds(NL * x, NL), :] = value

            block_transpose(NL, Q, load, store)
            turned = jnp.transpose(xform[...])[: M * C]
            strans[pl.ds(M * C * h, M * C), :] = turned.astype(BF16)

    xform = gsum

    def scatter_orders():
        for h in range(2):
            half = sback[pl.ds(M * C * h, M * C), :]
            xform[pl.ds(0, M * C), :] = half
            turned = jnp.transpose(xform[...])
            at = lax.broadcasted_iota(jnp.int32, (NL, RING), 1)
            for q in range(Q):
                row = jnp.where(at < M * C, turned[NL * q : NL * (q + 1)], 0.0)
                ring[q, :NL] = pltpu.roll(row, C * q, 1) if q else row

            def load(i, t):
                return ring[i, :NL, 128 * t : 128 * (t + 1)]

            def store(x, value, h=h):
                ring[M + M * h + x, :NL] = value

            block_transpose(NL, Q, load, store)

    def synth_lat(p):
        at = lanes(NL)
        tail = WIDTH[p] - 128
        start = C * PARTS[p][0]
        zero = jnp.zeros((NL, 128), F32)

        def main(kk):
            if p == 0:
                return ring[M + kk, :NL, :128]
            moved = pltpu.roll(ring[M + kk, :NL], RING - start, 1)[:, :128]
            return jnp.where(at < WIDTH[p], moved, zero)

        def end(kk, part):
            value = jnp.where(at < tail, ring[M + kk, :NL, 128:256], zero)
            return pltpu.roll(value, tail * part, 1) if part else value

        for i in range(16):
            second = main(16 + i) if i < 8 else zero
            if i >= 8 and tail > 0:
                second = end(i - 8, 0) + end(i, 1) + end(i + 8, 2)
            both = jnp.concatenate([main(i), second], axis=1)
            xbuf[pl.ds(NL * i, NL), :] = both.astype(BF16)
        moved = dot(permt[...], xbuf[pl.ds(0, 512), :]).astype(BF16)
        ls[p][2] = moved.reshape(NL, 16, 256)
        send_lat(2, p)

    def synth_lon(p):
        width = WIDTH[p]
        tail = width - 128
        wait_lat(2, p, lrs)
        got = lr[p][2]
        xbuf[pl.ds(0, 512), :128] = got[:, :, :128].reshape(512, 128)
        second = got[:, :, 128:].astype(F32)
        xbuf[pl.ds(512, 256), :128] = second[:, :8].reshape(256, 128).astype(BF16)
        if tail > 0:
            ends = second[:, 8:].reshape(256, 128)
            one = pltpu.roll(ends, 128 - tail, 1)
            two = pltpu.roll(ends, 128 - 2 * tail, 1)
            both = jnp.concatenate([ends.reshape(NL, 8, 128), one.reshape(NL, 8, 128)], axis=1)
            xbuf[pl.ds(0, 512), 128:] = both.reshape(512, 128).astype(BF16)
            xbuf[pl.ds(512, 256), 128:] = two.astype(BF16)
        else:
            xbuf[:, 128:] = jnp.zeros((768, 128), BF16)
        at = lax.broadcasted_iota(jnp.int32, (256, 256), 1)
        tiles = [None] * TILES[p]
        for g in range(GROUPS):
            base, shift = divmod(width * g, 128)
            value = dot(bwd[pl.ds(256 * g, 256), :], xbuf[...])
            value = jnp.where(at < width, value, 0.0)
            value = pltpu.roll(value, shift, 1) if shift else value
            for t in range(2):
                if base + t < TILES[p]:
                    piece = value[:, 128 * t : 128 * (t + 1)]
                    old = tiles[base + t]
                    tiles[base + t] = piece if old is None else old + piece
        for t in range(TILES[p]):
            zs[p][2, :, :, 128 * t : 128 * (t + 1)] = tiles[t].astype(BF16).reshape(NZ, 16, 128)
        send_lon(2, p)

    def unpack(p):
        first, rows = PARTS[p]
        wait_lon(2, p, zrs)

        def one(z, carry):
            for g in range(GROUPS):
                base, shift = divmod(WIDTH[p] * g, 128)
                window = zr[p][2, z, :, 128 * base : 128 * base + 256].astype(F32)
                wide = jnp.concatenate([window, jnp.zeros((16, 128), F32)], axis=1)
                move = lax.rem(C * (z + first) + RING - shift, RING)
                ring[z, 16 * g : 16 * (g + 1), :] = pltpu.roll(wide, move, 1)
            return carry

        lax.fori_loop(0, NZ, one, 0)
        for q in range(first, first + rows):
            merged = merge_blocks(
                N, lambda b, t: ring[(b - q) % NZ, :, 128 * t : 128 * (t + 1)]
            )
            merged = pltpu.roll(merged, RING - C * q, 1) if q else merged
            grad_out[q] = merged.astype(BF16)

    loads[0].wait()
    for p in range(2):
        pack(0, p)
    pl.semaphore_wait(barrier, NZ - 1 + NL - 1)
    for p in range(2):
        send_lon(0, p)
    loads[1].wait()
    for p in range(2):
        pack(1, p)
        send_lon(1, p)

    perm[...] = one_hot(512, lambda r: (r & (NL - 1)) * 16 + (r >> 5))
    permt[...] = one_hot(512, lambda r: (r & 15) * NL + (r >> 4))
    order = one_hot(LATS, lambda r: (r & (NL - 1)) * Q + (r >> 5))
    loads[2].wait()

    def reorder(m, carry):
        legp[m] = dot(order, leg[m]).astype(BF16)
        return carry

    lax.fori_loop(0, M, reorder, 0)
    loads[5].wait()
    gain = []
    for r in range(2):
        wide = jnp.concatenate(
            [filt[:, r, :], jnp.zeros((DEGREES, 128 - C), F32)], axis=1
        )
        gain.append(jnp.transpose(wide)[:C])
    loads[3].wait()
    loads[4].wait()

    for p in range(2):
        analyse_lon(0, p)
    analyse_lat(0)

    def filter_order(m, carry):
        rows = pl.ds(pl.multiple_of(2 * C * m, 16), 2 * C)
        got = dot(strans[rows, :], legp[m])
        coef[m] = got
        re, im = got[:C], got[C:]
        back = jnp.concatenate(
            [gain[0] * re + gain[1] * im, gain[0] * im - gain[1] * re], axis=0
        ).astype(BF16)
        sback[rows, :] = lax.dot_general(
            back, legp[m], (((1,), (1,)), ((), ())), preferred_element_type=F32
        )
        return carry

    lax.fori_loop(0, M, filter_order, 0)
    scatter_orders()
    for p in range(2):
        synth_lat(p)
    for p in range(2):
        synth_lon(p)

    for p in range(2):
        analyse_lon(1, p)
    analyse_lat(1)
    acc[...] = jnp.zeros_like(acc)

    def correlate(m, carry):
        rows = pl.ds(pl.multiple_of(2 * C * m, 16), 2 * C)
        got = dot(strans[rows, :], legp[m])
        in_re, in_im = got[:C], got[C:]
        cot_re, cot_im = coef[m, :C], coef[m, C:]
        acc[pl.ds(0, C), :] += in_re * cot_re + in_im * cot_im
        acc[pl.ds(C, C), :] += in_re * cot_im - in_im * cot_re
        return carry

    lax.fori_loop(0, M, correlate, 0)
    gs[...] = jnp.transpose(acc[...])

    def send_sum(s, carry):
        to = lax.rem(lat + NL - 1 - s, NL)
        start = pl.multiple_of(Q * to - 4 * lax.rem(to, 2), 8)
        pltpu.make_async_remote_copy(
            src_ref=gs.at[pl.ds(start, 16)],
            dst_ref=gr.at[lat],
            send_sem=gss,
            recv_sem=grs,
            device_id=(to, lon),
            device_id_type=MESH,
        ).start()
        return carry

    lax.fori_loop(0, NL - 1, send_sum, 0)
    start = pl.multiple_of(Q * lat - 4 * lax.rem(lat, 2), 8)
    own = pltpu.make_async_copy(gs.at[pl.ds(start, 16)], gr.at[lat], own_sem.at[2])
    own.start()
    own.wait()
    some = gr.at[pl.ds(0, NL - 1)]
    pltpu.make_async_copy(some, some, grs).wait()
    total = jnp.sum(gr[...], axis=0)
    total = jnp.where(lax.rem(lat, 2) == 1, total[4:16], total[:12])
    filt_out[:, 0, :] = total[:, :C]
    filt_out[:, 1, :] = total[:, C : 2 * C]

    for p in range(2):
        unpack(p)

    for phase in range(3):
        for p in range(2):
            wait_lon(phase, p, zss)
            wait_lat(phase, p, lss)
    pltpu.make_async_copy(some, some, gss).wait()


def local(grid_in, grid_cot, legendre, filters):
    fwd, bwd = fourier_tables()
    vmem = pltpu.VMEM
    any_space = pl.BlockSpec(memory_space=pl.ANY)
    return pl.pallas_call(
        kernel,
        out_shape=(
            jax.ShapeDtypeStruct((Q, N, CHANNELS), BF16),
            jax.ShapeDtypeStruct((Q, 2, C), F32),
        ),
        in_specs=[any_space] * 6,
        out_specs=(pl.BlockSpec(memory_space=vmem), pl.BlockSpec(memory_space=vmem)),
        scratch_shapes=[
            vmem((2, Q, N, CHANNELS), BF16),
            vmem((M, LATS, DEGREES), BF16),
            vmem((M, LATS, DEGREES), BF16),
            vmem((DEGREES, 2, C), F32),
            vmem((2 * DEGREES, LONS), BF16),
            vmem((LONS, 2 * DEGREES), BF16),
            vmem((512, 512), BF16),
            vmem((512, 512), BF16),
            vmem((3 * M, N, RING), F32),
            vmem((768, 256), BF16),
            vmem((768, 256), F32),
            vmem((2 * M * C, LATS), BF16),
            vmem((2 * M * C, LATS), F32),
            vmem((M, 2 * C, DEGREES), F32),
            vmem((128, DEGREES), F32),
            vmem((RING, LATS), F32),
            vmem((3, NZ, 16, 128 * TILES[0]), BF16),
            vmem((3, NZ, 16, 128 * TILES[1]), BF16),
            vmem((3, NZ, 16, 128 * TILES[0]), BF16),
            vmem((3, NZ, 16, 128 * TILES[1]), BF16),
            vmem((3, NL, 16, 256), BF16),
            vmem((3, NL, 16, 256), BF16),
            vmem((3, NL, 16, 256), BF16),
            vmem((3, NL, 16, 256), BF16),
            vmem((DEGREES, 128), F32),
            vmem((NL, 16, 128), F32),
            pltpu.SemaphoreType.DMA((6,)),
            pltpu.SemaphoreType.DMA((3,)),
            pltpu.SemaphoreType.DMA((3, 2)),
            pltpu.SemaphoreType.DMA((3, 2)),
            pltpu.SemaphoreType.DMA((3, 2)),
            pltpu.SemaphoreType.DMA((3, 2)),
            pltpu.SemaphoreType.DMA,
            pltpu.SemaphoreType.DMA,
        ],
        compiler_params=pltpu.CompilerParams(
            collective_id=0, has_side_effects=True, vmem_limit_bytes=56 * 1024 * 1024
        ),
    )(grid_in, grid_cot, legendre, filters, jnp.asarray(fwd), jnp.asarray(bwd))


def solution(mesh):
    return jax.shard_map(
        local,
        mesh=mesh,
        in_specs=(
            P("lat", "lon", None),
            P("lat", "lon", None),
            P("lat", None, None),
            P(None, None, "lon"),
        ),
        out_specs=(P("lat", "lon", None), P("lat", None, "lon")),
        check_vma=False,
    )
```

time: 372 us -> 95.3 us (0.26); the launches traced: 367 us -> 95 us
  waiting for transfers between devices: 148 us -> 0 us
  local copies, waits for them, and re-layouts: 110 us -> 4.93 us
  Pallas kernels: 0 us -> 89.5 us
  starting transfers between devices: 55.4 us -> 0 us
  blocking collectives: 18.2 us -> 0 us
  between operations: 15.3 us -> 0.64 us
  matrix products: 12 us -> 0 us
  other arithmetic: 7.63 us -> 0 us
    unnamed x2 -> x0, waiting for transfers between devices: 132 us -> none
    pallas_call x0 -> x1, Pallas kernels: none -> 89.5 us  [local(): pl.pallas_call(kernel, out_shape=(jax.ShapeDtypeStruct((Q, N, CHANNELS),...]
    all_to_all x5 -> x0, starting transfers between devices: 55.3 us -> none  [the longest x1 15.7 us: local(): lax.all_to_all(grid_cot, 'lon', split_axis=2, concat_axis=1, tiled=True)]
    unnamed x47 -> x3, local copies, waits for them, and re-layouts: 55 us -> 4.93 us
    all_to_all x9 -> x0, local copies, waits for them, and re-layouts: 24.5 us -> none  [the longest x2 6.67 us: local(): lax.all_to_all(order_spec, 'lat', split_axis=0, concat_axis=2, tiled=True)]
    all_to_all x1 -> x0, blocking collectives: 18.2 us -> none  [local(): lax.all_to_all(order_spec, 'lat', split_axis=0, concat_axis=2, tiled=True)]
    all_to_all x5 -> x0, waiting for transfers between devices: 16.3 us -> none  [the longest x1 16.3 us: local(): lax.all_to_all(grid_cot, 'lon', split_axis=2, concat_axis=1, tiled=True)]
    reshape x3 -> x0, local copies, waits for them, and re-layouts: 15.7 us -> none  [the longest x2 12.7 us: analyse(): shaped = spectra.reshape(lat_rows, chan_count, orders_dev, 2)]
  transfers between devices with their start and end apart: 6 -> 0, of which waited for: 2 -> 0; matrix products, arithmetic and copies ran while one was open for 17% -> 0% of each run, Pallas kernels for 0% -> 0%
where the time goes in v1:
time: 95.3 us; the launch traced here: 95 us
  Pallas kernels  89.5 us (94%)
  local copies, waits for them, and re-layouts  4.93 us (5%)
    pallas_call x1, Pallas kernels, local(): pl.pallas_call(kernel, out_shape=(jax.ShapeDtypeStruct((Q, N, CHANNELS),...  89.5 us
    unnamed x3, local copies, waits for them, and re-layouts  4.93 us

profile of v1, /device:TPU:1, one launch (start us, length us, event | category | flops | bytes accessed | tf_op | source)
XLA Modules:
  0.0 95.0 jit_solution(17771426196060962763)
XLA Ops:
  0.6 1.8 %copy.8.filt_hbm = f32[384,2,24]{2,1,0:T(2,128)} copy(f32[384,2,24]{0,2,1:T(8,128)} %param.9) | data formatting | bytes 147456 | tf_op args[3]
  2.4 89.5 %shard_map.77 = (bf16[12,48,384]{2,1,0:T(8,128)(2,1)}, f32[12,2,24]{2,1,0:T(2,128)}) custom-call(bf16[12,48,384]{2,1,0:T(8,128)(2,1)} %in_hbm.1, bf16[12,48,384]{2,1,0:T(8,128)(2,1)} %cot_hbm.1, bf16[12,384,384]{2,1,0:T(8,128)(2,1)} %leg_hbm.1, f32[384,2,24]{2,1,0:T(2,128)} %copy.8.filt_hbm, bf16[768,768]{1,0:T(8,128)(2,1)} %constant.4.clone.fwd_hbm, ...), custom_call_target="tpu_custom_call" | custom-call | tf_op jit(solution)/shard_map/pallas_call | solution.py:470
  91.9 1.8 %copy.11 = bf16[12,48,384]{2,1,0:T(8,128)(2,1)} copy(bf16[12,48,384]{2,1,0:T(8,128)(2,1)} %get-tuple-element.4) | data formatting | bytes 884736
  93.7 1.3 %copy.12 = f32[12,2,24]{2,1,0:T(2,128)} copy(f32[12,2,24]{2,1,0:T(2,128)} %get-tuple-element.5) | data formatting | bytes 4608

commit v2 on v1

v2 whole, which is shorter than its diff:
```python
import math

import jax
import jax.numpy as jnp
import ml_dtypes
import numpy as np
from jax import lax
from jax.experimental import pallas as pl
from jax.experimental.pallas import tpu as pltpu
from jax.sharding import PartitionSpec as P

MESH = pl.DeviceIdType.MESH
BF16 = jnp.bfloat16
F32 = jnp.float32

NZ, NL = 16, 32
LATS, LONS, DEGREES, CHANNELS = 384, 768, 384, 384
Q, N, C = LATS // NL, LONS // NZ, CHANNELS // NZ
M = DEGREES // NL
K = 2 * M
RING = 384
GROUPS = N // 16
SLOT = 16

PARTS = ((0, 14), (14, 10))
WIDTH = tuple(Q * count for _, count in PARTS)
TILES = tuple(-(-GROUPS * w // 128) for w in WIDTH)


def fourier_tables():
    points = np.arange(LONS, dtype=np.int64)[:, None]
    order = np.arange(DEGREES, dtype=np.int64)[None, :]
    phases = (points * order) % LONS
    angles = phases.astype(np.float32) * np.float32(2.0 * math.pi / LONS)
    pair = np.stack([np.cos(angles), -np.sin(angles)], axis=2) * np.float32(LONS ** (-0.5))
    table = pair.reshape(LONS, 2 * DEGREES).astype(ml_dtypes.bfloat16)
    n_of = np.arange(LONS).reshape(NZ, GROUPS, 16).transpose(1, 0, 2).reshape(-1)
    k = np.arange(2 * DEGREES).reshape(NL, 2 * M)
    k_of = np.concatenate([k[:, :16].reshape(-1), k[:, 16:].reshape(-1)])
    back = table[n_of][:, k_of]
    return np.ascontiguousarray(back.T), np.ascontiguousarray(back)


def lanes(rows):
    return lax.broadcasted_iota(jnp.int32, (rows, 128), 1)


def merge(rows, start, step, count, pick):
    at = lanes(rows)
    tiles = []
    for t in range(start // 128, (start + step * count - 1) // 128 + 1):
        value = None
        for i in range(count):
            low, high = start + step * i - 128 * t, start + step * (i + 1) - 128 * t
            if high <= 0 or low >= 128:
                continue
            block = pick(i, t)
            value = block if value is None else jnp.where(at >= low, block, value)
        tiles.append(value)
    return tiles


def shift_left(tiles, shift):
    wide = jnp.concatenate(tiles, axis=1) if len(tiles) > 1 else tiles[0]
    size = 128 * len(tiles)
    return pltpu.roll(wide, (size - shift) % size, 1) if shift % size else wide


def one_hot(size, column_of):
    row = lax.broadcasted_iota(jnp.int32, (size, size), 0)
    column = lax.broadcasted_iota(jnp.int32, (size, size), 1)
    return jnp.where(column == column_of(row), 1.0, 0.0).astype(BF16)


def dot(a, b):
    return jnp.dot(a, b, preferred_element_type=F32)


def kernel(
    in_hbm, cot_hbm, leg_hbm, filt_hbm, fwd_hbm, bwd_hbm,
    grad_out, filt_out,
    grid, leg, legp, filt, fwd, bwd, perm, permt, ring, pbuf, gain, xbuf, dbuf, xform, strans, sback, coef, acc,
    zs_a, zs_b, zr_a, zr_b, ls_a, ls_b, lr_a, lr_b, gs, gr,
    load_sem, own_sem, zss, zrs, lss, lrs, gss, grs,
):
    lat, lon = lax.axis_index("lat"), lax.axis_index("lon")
    zs, zr, ls, lr = (zs_a, zs_b), (zr_a, zr_b), (ls_a, ls_b), (lr_a, lr_b)

    barrier = pltpu.get_barrier_semaphore()
    for d in (8, 7, 9, 6, 10, 5, 11, 4, 12, 3, 13, 2, 14, 1, 15):
        pl.semaphore_signal(
            barrier, inc=1, device_id=(lat, lax.rem(lon + d, NZ)), device_id_type=MESH
        )

    def greet(d, carry):
        pl.semaphore_signal(
            barrier, inc=1, device_id=(lax.rem(lat + d, NL), lon), device_id_type=MESH
        )
        return carry

    lax.fori_loop(1, NL, greet, 0)
    loads = [
        pltpu.make_async_copy(cot_hbm, grid.at[0], load_sem.at[0]),
        pltpu.make_async_copy(in_hbm, grid.at[1], load_sem.at[1]),
        pltpu.make_async_copy(leg_hbm, leg, load_sem.at[2]),
        pltpu.make_async_copy(fwd_hbm, fwd, load_sem.at[3]),
        pltpu.make_async_copy(bwd_hbm, bwd, load_sem.at[4]),
        pltpu.make_async_copy(filt_hbm, filt, load_sem.at[5]),
    ]
    for load in loads:
        load.start()
    def send_lon(phase, p):
        def step(s, carry):
            half = lax.div(s + 1, 2)
            d = jnp.where(lax.rem(s, 2) == 0, 8 + half, 8 - half)
            to = lax.rem(lon + d, NZ)
            pltpu.make_async_remote_copy(
                src_ref=zs[p].at[phase, to],
                dst_ref=zr[p].at[phase, lon],
                send_sem=zss.at[phase, p],
                recv_sem=zrs.at[phase, p],
                device_id=(lat, to),
                device_id_type=MESH,
            ).start()
            return carry

        lax.fori_loop(0, NZ - 1, step, 0)
        zr[p][phase, lon] = zs[p][phase, lon]

    def wait_lon(phase, p, sem):
        some = zr[p].at[phase, pl.ds(0, NZ - 1)]
        pltpu.make_async_copy(some, some, sem.at[phase, p]).wait()

    def send_lat(phase, p):
        def step(s, carry):
            to = lat ^ (NL - 1 - s)
            pltpu.make_async_remote_copy(
                src_ref=ls[p].at[phase, to],
                dst_ref=lr[p].at[phase, lat],
                send_sem=lss.at[phase, p],
                recv_sem=lrs.at[phase, p],
                device_id=(to, lon),
                device_id_type=MESH,
            ).start()
            return carry

        lax.fori_loop(0, NL - 1, step, 0)
        lr[p][phase, lat] = ls[p][phase, lat]

    def wait_lat(phase, p, sem):
        some = lr[p].at[phase, pl.ds(0, NL - 1)]
        pltpu.make_async_copy(some, some, sem.at[phase, p]).wait()

    def pack(a, p):
        first, count = PARTS[p]
        at = lanes(16)
        for q in range(Q):
            wide = grid[a, q]
            pbuf[q] = pltpu.roll(wide, count * q, 1) if q else wide
        for z in range(NZ):
            start = C * z + first
            moved = jnp.concatenate(
                merge(N, start, count, Q, lambda q, t: pbuf[q, :, 128 * (t % 3) : 128 * (t % 3) + 128]),
                axis=1,
            )
            size = moved.shape[1]
            if size == 128:
                moved = jnp.concatenate([moved, moved], axis=1)
                size = 256
            tiles = [None] * (TILES[p] + 1)
            for g in range(GROUPS):
                base, shift = divmod(WIDTH[p] * g, 128)
                turn = (shift - start % 128) % size
                rows = moved[16 * g : 16 * (g + 1)]
                rows = pltpu.roll(rows, turn, 1) if turn else rows
                old = tiles[base]
                tiles[base] = rows[:, :128] if old is None else jnp.where(at >= shift, rows[:, :128], old)
                tiles[base + 1] = rows[:, 128:256]
            zs[p][a, z] = jnp.concatenate(tiles[: TILES[p]], axis=1)

    def analyse_lon(a, p):
        width = WIDTH[p]
        wait_lon(a, p, zrs)
        for g in range(GROUPS):
            base, shift = divmod(width * g, 128)
            window = zr[p][a, :, :, 128 * base : 128 * base + 256].reshape(256, 256)
            if shift:
                window = pltpu.roll(window.astype(F32), 256 - shift, 1).astype(BF16)
            xbuf[pl.ds(256 * g, 256), :] = window
        for r in range(3):
            dbuf[pl.ds(256 * r, 256), :] = dot(fwd[pl.ds(256 * r, 256), :], xbuf[...])
        low = dbuf[pl.ds(0, 512), :128].reshape(NL, 16, 128)
        ls[p][a, :, :, :128] = low.astype(BF16)
        high = dbuf[pl.ds(512, 256), :128].reshape(NL, 8, 128)
        tail = width - 128
        if tail > 0:
            at = lax.broadcasted_iota(jnp.int32, (512, 128), 1)
            first = jnp.where(at < tail, dbuf[pl.ds(0, 512), 128:], 0.0).reshape(NL, 16, 128)
            last = jnp.where(at[:256] < tail, dbuf[pl.ds(512, 256), 128:], 0.0)
            ends = first[:, :8] + (
                pltpu.roll(first[:, 8:].reshape(256, 128), tail, 1)
                + pltpu.roll(last, 2 * tail, 1)
            ).reshape(NL, 8, 128)
        else:
            ends = jnp.zeros((NL, 8, 128), F32)
        ls[p][a, :, :, 128:] = jnp.concatenate([high, ends], axis=1).astype(BF16)
        send_lat(a, p)

    def analyse_lat(a, p):
        count = PARTS[p][1]
        tail = WIDTH[p] - 128
        at = lanes(NL)
        wait_lat(a, p, lrs)
        dbuf[pl.ds(0, 512), :] = dot(perm[...], lr[p][a].reshape(512, 256))
        for kk in range(K):
            base, shift = divmod(SLOT * kk, 128)
            i, t = (kk, 0) if kk < 16 else (kk - 16, 1)
            main = dbuf[pl.ds(NL * i, NL), 128 * t : 128 * (t + 1)]
            main = pltpu.roll(main, shift, 1) if shift else main
            ring[kk, :, :128] = main
            if tail > 0:
                end = dbuf[pl.ds(NL * (8 + kk % 8), NL), 128:]
                turn = (shift - tail * (kk // 8)) % 128
                end = pltpu.roll(end, turn, 1) if turn else end
                ring[kk, :, 128:256] = jnp.where(at < shift, main, end) if shift else end
                ring[kk, :, 256:384] = end
            else:
                ring[kk, :, 128:256] = main
        for q in range(Q):
            start = count * q

            def pick(kk, t):
                t -= SLOT * kk // 128
                return ring[kk, :, 128 * t : 128 * (t + 1)]

            tiles = merge(NL, start, SLOT, K, pick)
            xform[pl.ds(NL * q, NL), :] = shift_left(tiles, start % 128)[:, : SLOT * K]
        strans[...] = jnp.transpose(xform[...]).astype(BF16)

    def synth_lat(p):
        count = PARTS[p][1]
        tail = WIDTH[p] - 128
        at = lanes(NL)
        xform[...] = jnp.transpose(sback[...])
        blank = jnp.zeros((NL, 128), F32)
        for q in range(Q):
            row = jnp.concatenate([xform[pl.ds(NL * q, NL), :], blank], axis=1)
            shift = count * q % 128
            ring[q] = pltpu.roll(row, shift, 1) if shift else row

        def column(kk):
            def pick(q, t):
                t -= count * q // 128
                return ring[q, :, 128 * t : 128 * (t + 1)]

            tiles = merge(NL, SLOT * kk, count, Q, pick)
            return shift_left(tiles, SLOT * kk % 128)

        for i in range(16):
            low = column(i)
            ring[Q + i % 8, :, 128 * (i // 8) : 128 * (i // 8 + 1)] = low[:, :128]
            if tail > 0:
                done = low[:, 128:256]
                if i < 8:
                    ring[Q + i, :, 256:384] = done
                else:
                    old = ring[Q + i - 8, :, 256:384]
                    ring[Q + i - 8, :, 256:384] = jnp.where(at >= tail, pltpu.roll(done, tail, 1), old)
        for i in range(8):
            high = column(16 + i)
            low = ring[Q + i, :, :128]
            xbuf[pl.ds(NL * i, NL), :] = jnp.concatenate([low, high[:, :128]], axis=1).astype(BF16)
            ends = blank
            if tail > 0:
                ends = jnp.where(
                    at >= 2 * tail, pltpu.roll(high[:, 128:256], 2 * tail, 1), ring[Q + i, :, 256:384]
                )
            low = ring[Q + i, :, 128:256]
            xbuf[pl.ds(NL * (8 + i), NL), :] = jnp.concatenate([low, ends], axis=1).astype(BF16)
        moved = dot(permt[...], xbuf[pl.ds(0, 512), :]).astype(BF16)
        ls[p][2] = moved.reshape(NL, 16, 256)
        send_lat(2, p)

    def synth_lon(p):
        width = WIDTH[p]
        tail = width - 128
        wait_lat(2, p, lrs)
        got = lr[p][2]
        xbuf[pl.ds(0, 512), :128] = got[:, :, :128].reshape(512, 128)
        second = got[:, :, 128:].astype(F32)
        xbuf[pl.ds(512, 256), :128] = second[:, :8].reshape(256, 128).astype(BF16)
        if tail > 0:
            ends = second[:, 8:].reshape(256, 128)
            one = pltpu.roll(ends, 128 - tail, 1)
            two = pltpu.roll(ends, 128 - 2 * tail, 1)
            both = jnp.concatenate([ends.reshape(NL, 8, 128), one.reshape(NL, 8, 128)], axis=1)
            xbuf[pl.ds(0, 512), 128:] = both.reshape(512, 128).astype(BF16)
            xbuf[pl.ds(512, 256), 128:] = two.astype(BF16)
        else:
            xbuf[:, 128:] = jnp.zeros((768, 128), BF16)
        at = lax.broadcasted_iota(jnp.int32, (256, 256), 1)
        tiles = [None] * TILES[p]
        for g in range(GROUPS):
            base, shift = divmod(width * g, 128)
            value = dot(bwd[pl.ds(256 * g, 256), :], xbuf[...])
            value = jnp.where(at < width, value, 0.0)
            value = pltpu.roll(value, shift, 1) if shift else value
            for t in range(2):
                if base + t < TILES[p]:
                    piece = value[:, 128 * t : 128 * (t + 1)]
                    old = tiles[base + t]
                    tiles[base + t] = piece if old is None else old + piece
        for t in range(TILES[p]):
            zs[p][2, :, :, 128 * t : 128 * (t + 1)] = tiles[t].astype(BF16).reshape(NZ, 16, 128)
        send_lon(2, p)

    def unpack(p):
        first, count = PARTS[p]
        wait_lon(2, p, zrs)
        for z in range(NZ):
            for g in range(GROUPS):
                base, shift = divmod(WIDTH[p] * g, 128)
                window = [zr[p][2, z, :, 128 * t : 128 * (t + 1)] for t in range(base, min(base + 2, TILES[p]))]
                window += [window[-1]] * (3 - len(window))
                turn = (C * z + first - shift) % RING
                wide = jnp.concatenate(window, axis=1)
                pbuf[z, 16 * g : 16 * (g + 1), :] = pltpu.roll(wide, turn, 1) if turn else wide
        at = lanes(N)
        for q in range(Q):
            start = first + count * q
            tiles = []
            for t in range(3):
                low = 128 * t - start
                z = low // C
                value = pbuf[z % NZ, :, 128 * t : 128 * (t + 1)]
                while C * (z + 1) - low < 128:
                    z += 1
                    value = jnp.where(
                        at >= C * z - low, pbuf[z % NZ, :, 128 * t : 128 * (t + 1)], value
                    )
                tiles.append(value)
            whole = shift_left(tiles, count * q)
            if p == 0:
                grad_out[q] = whole
            else:
                for t in range(3):
                    span = slice(128 * t, 128 * (t + 1))
                    inner = lax.rem(at + 128 * t, C)
                    grad_out[q, :, span] = jnp.where(inner < first, grad_out[q, :, span], whole[:, span])

    loads[0].wait()
    pack(0, 0)
    pl.semaphore_wait(barrier, NZ - 1 + NL - 1)
    send_lon(0, 0)
    pack(0, 1)
    send_lon(0, 1)
    loads[1].wait()
    pack(1, 0)
    send_lon(1, 0)
    pack(1, 1)
    send_lon(1, 1)

    perm[...] = one_hot(512, lambda r: (r & (NL - 1)) * 16 + (r >> 5))
    permt[...] = one_hot(512, lambda r: (r & 15) * NL + (r >> 4))
    order = one_hot(LATS, lambda r: (r & (NL - 1)) * Q + (r >> 5))
    loads[2].wait()

    def reorder(m, carry):
        legp[m] = dot(order, leg[m]).astype(BF16)
        return carry

    lax.fori_loop(0, M, reorder, 0, unroll=2)
    loads[5].wait()
    gain[0] = filt[:, :SLOT]
    for r in range(2):
        first, count = PARTS[1]
        gain[1, r, :count] = filt[r, first:]
        gain[1, r, count:] = jnp.zeros((SLOT - count, DEGREES), F32)
    loads[3].wait()
    loads[4].wait()

    def spectrum(m):
        rows = pl.ds(pl.multiple_of(2 * SLOT * m, 2 * SLOT), 2 * SLOT)
        return dot(strans[rows, :], legp[m])

    def filter_cot(p):
        def analyse(m, carry):
            coef[p, m] = spectrum(m)
            return carry

        lax.fori_loop(0, M, analyse, 0, unroll=4)

        def synth(m, carry):
            re, im = coef[p, m, :SLOT], coef[p, m, SLOT:]
            back = jnp.concatenate(
                [gain[p, 0] * re + gain[p, 1] * im, gain[p, 0] * im - gain[p, 1] * re], axis=0
            ).astype(BF16)
            rows = pl.ds(pl.multiple_of(2 * SLOT * m, 2 * SLOT), 2 * SLOT)
            sback[rows, :] = lax.dot_general(
                back, legp[m], (((1,), (1,)), ((), ())), preferred_element_type=F32
            )
            return carry

        lax.fori_loop(0, M, synth, 0, unroll=4)

    def correlate(p):
        def one(m, carry):
            got = spectrum(m)
            in_re, in_im = got[:SLOT], got[SLOT:]
            cot_re, cot_im = coef[p, m, :SLOT], coef[p, m, SLOT:]
            acc[pl.ds(2 * SLOT * p, SLOT), :] += in_re * cot_re + in_im * cot_im
            acc[pl.ds(2 * SLOT * p + SLOT, SLOT), :] += in_re * cot_im - in_im * cot_re
            return carry

        lax.fori_loop(0, M, one, 0, unroll=4)

    acc[...] = jnp.zeros_like(acc)
    analyse_lon(0, 0)
    analyse_lat(0, 0)
    analyse_lon(0, 1)
    filter_cot(0)
    synth_lat(0)
    analyse_lat(0, 1)
    filter_cot(1)
    synth_lat(1)
    synth_lon(0)
    analyse_lon(1, 0)
    synth_lon(1)
    analyse_lon(1, 1)
    analyse_lat(1, 0)
    correlate(0)
    analyse_lat(1, 1)
    correlate(1)
    gs[...] = jnp.transpose(acc[...])

    def send_sum(s, carry):
        to = lat ^ (NL - 1 - s)
        start = pl.multiple_of(Q * to - 4 * lax.rem(to, 2), 8)
        pltpu.make_async_remote_copy(
            src_ref=gs.at[pl.ds(start, 16)],
            dst_ref=gr.at[lat],
            send_sem=gss,
            recv_sem=grs,
            device_id=(to, lon),
            device_id_type=MESH,
        ).start()
        return carry

    lax.fori_loop(0, NL - 1, send_sum, 0)
    start = pl.multiple_of(Q * lat - 4 * lax.rem(lat, 2), 8)
    own = pltpu.make_async_copy(gs.at[pl.ds(start, 16)], gr.at[lat], own_sem.at[0])
    own.start()
    own.wait()
    some = gr.at[pl.ds(0, NL - 1)]
    unpack(0)
    pltpu.make_async_copy(some, some, grs).wait()
    total = jnp.sum(gr[...], axis=0)
    total = jnp.where(lax.rem(lat, 2) == 1, total[4:16], total[:12])
    for r in range(2):
        for p in range(2):
            first, count = PARTS[p]
            low = 2 * SLOT * p + SLOT * r
            filt_out[:, r, first : first + count] = total[:, low : low + count]
    unpack(1)

    for phase in range(3):
        for p in range(2):
            wait_lon(phase, p, zss)
            wait_lat(phase, p, lss)
    pltpu.make_async_copy(some, some, gss).wait()


def hand_over(grad_in, filt_in, grad_out, filt_out):
    grad_out[...] = grad_in[...]
    filt_out[...] = filt_in[...]


def local(grid_in, grid_cot, legendre, filters):
    fwd, bwd = fourier_tables()
    vmem = pltpu.VMEM
    any_space = pl.BlockSpec(memory_space=pl.ANY)
    outs = pl.pallas_call(
        kernel,
        out_shape=(
            jax.ShapeDtypeStruct((Q, N, CHANNELS), BF16),
            jax.ShapeDtypeStruct((Q, 2, C), F32),
        ),
        in_specs=[any_space] * 6,
        out_specs=(pl.BlockSpec(memory_space=vmem), pl.BlockSpec(memory_space=vmem)),
        scratch_shapes=[
            vmem((2, Q, N, CHANNELS), BF16),
            vmem((M, LATS, DEGREES), BF16),
            vmem((M, LATS, DEGREES), BF16),
            vmem((2, C, DEGREES), F32),
            vmem((2 * DEGREES, LONS), BF16),
            vmem((LONS, 2 * DEGREES), BF16),
            vmem((512, 512), BF16),
            vmem((512, 512), BF16),
            vmem((K, NL, 512), F32),
            vmem((NZ, N, RING), BF16),
            vmem((2, 2, SLOT, DEGREES), F32),
            vmem((768, 256), BF16),
            vmem((768, 256), F32),
            vmem((LATS, SLOT * K), F32),
            vmem((SLOT * K, LATS), BF16),
            vmem((SLOT * K, LATS), F32),
            vmem((2, M, 2 * SLOT, DEGREES), F32),
            vmem((128, DEGREES), F32),
            vmem((3, NZ, 16, 128 * TILES[0]), BF16),
            vmem((3, NZ, 16, 128 * TILES[1]), BF16),
            vmem((3, NZ, 16, 128 * TILES[0]), BF16),
            vmem((3, NZ, 16, 128 * TILES[1]), BF16),
            vmem((3, NL, 16, 256), BF16),
            vmem((3, NL, 16, 256), BF16),
            vmem((3, NL, 16, 256), BF16),
            vmem((3, NL, 16, 256), BF16),
            vmem((DEGREES, 128), F32),
            vmem((NL, 16, 128), F32),
            pltpu.SemaphoreType.DMA((6,)),
            pltpu.SemaphoreType.DMA((1,)),
            pltpu.SemaphoreType.DMA((3, 2)),
            pltpu.SemaphoreType.DMA((3, 2)),
            pltpu.SemaphoreType.DMA((3, 2)),
            pltpu.SemaphoreType.DMA((3, 2)),
            pltpu.SemaphoreType.DMA,
            pltpu.SemaphoreType.DMA,
        ],
        compiler_params=pltpu.CompilerParams(
            collective_id=0, has_side_effects=True, vmem_limit_bytes=56 * 1024 * 1024
        ),
    )(
        grid_in, grid_cot, legendre, jnp.transpose(filters, (1, 2, 0)), jnp.asarray(fwd), jnp.asarray(bwd)
    )
    return pl.pallas_call(
        hand_over,
        out_shape=tuple(jax.ShapeDtypeStruct(out.shape, out.dtype) for out in outs),
        in_specs=[pl.BlockSpec(memory_space=vmem)] * 2,
        out_specs=(pl.BlockSpec(memory_space=vmem), pl.BlockSpec(memory_space=vmem)),
    )(*outs)


def solution(mesh):
    return jax.shard_map(
        local,
        mesh=mesh,
        in_specs=(
            P("lat", "lon", None),
            P("lat", "lon", None),
            P("lat", None, None),
            P(None, None, "lon"),
        ),
        out_specs=(P("lat", "lon", None), P("lat", None, "lon")),
        check_vma=False,
    )
```

time: 95.3 us -> 81 us (0.85)
  Pallas kernels: 89.5 us -> 80.2 us
  local copies, waits for them, and re-layouts: 4.93 us -> 0 us
    pallas_call x1, Pallas kernels: 89.5 us -> 78.4 us  [local(): pl.pallas_call(kernel, out_shape=(jax.ShapeDtypeStruct((Q, N, CHANNELS),...]
    unnamed x3 -> x0, local copies, waits for them, and re-layouts: 4.93 us -> none
    pallas_call x0 -> x1, Pallas kernels: none -> 1.82 us  [local(): pl.pallas_call(hand_over, out_shape=tuple((jax.ShapeDtypeStruct(out.shape...]
where the time goes in v2:
time: 81 us; the launch traced here: 80.8 us
  Pallas kernels  80.2 us (99%)
    pallas_call x1, Pallas kernels, local(): pl.pallas_call(kernel, out_shape=(jax.ShapeDtypeStruct((Q, N, CHANNELS),...  78.4 us
    pallas_call x1, Pallas kernels, local(): pl.pallas_call(hand_over, out_shape=tuple((jax.ShapeDtypeStruct(out.shape...  1.82 us

profile of v2, /device:TPU:1, one launch (start us, length us, event | category | flops | bytes accessed | tf_op | source)
XLA Modules:
  0.0 80.8 jit_solution(10523820774139647334)
XLA Ops:
  0.6 78.4 %shard_map.77 = (bf16[12,48,384]{2,1,0:T(8,128)(2,1)}, f32[12,2,24]{2,1,0:T(2,128)}) custom-call(bf16[12,48,384]{2,1,0:T(8,128)(2,1)} %in_hbm.1, bf16[12,48,384]{2,1,0:T(8,128)(2,1)} %cot_hbm.1, bf16[12,384,384]{2,1,0:T(8,128)(2,1)} %leg_hbm.1, f32[2,24,384]{2,1,0:T(8,128)} %bitcast.1, bf16[768,768]{1,0:T(8,128)(2,1)} %constant.4.clone.fwd_hbm, ...), custom_call_target="tpu_custom_call" | custom-call | tf_op jit(solution)/shard_map/pallas_call | solution.py:482
  79.0 1.8 %shard_map.78 = (bf16[12,48,384]{2,1,0:T(8,128)(2,1)}, f32[12,2,24]{2,1,0:T(2,128)}) custom-call(bf16[12,48,384]{2,1,0:T(8,128)(2,1)} %get-tuple-element.4.grad_in, f32[12,2,24]{2,1,0:T(2,128)} %get-tuple-element.5.filt_in), custom_call_target="tpu_custom_call" | custom-call | tf_op jit(solution)/shard_map/pallas_call | solution.py:534

commit v3 on v2

--- a/solution.py
+++ b/solution.py
@@ -81,24 +81,28 @@
     grad_out, filt_out,
     grid, leg, legp, filt, fwd, bwd, perm, permt, ring, pbuf, gain, xbuf, dbuf, xform, strans, sback, coef, acc,
     zs_a, zs_b, zr_a, zr_b, ls_a, ls_b, lr_a, lr_b, gs, gr,
-    load_sem, own_sem, zss, zrs, lss, lrs, gss, grs,
+    load_sem, own_sem, zss, zrs, lss, lrs, gss, grs, far_sem, col_sem,
 ):
     lat, lon = lax.axis_index("lat"), lax.axis_index("lon")
     zs, zr, ls, lr = (zs_a, zs_b), (zr_a, zr_b), (ls_a, ls_b), (lr_a, lr_b)
 
+    def ring_peer(d):
+        return (lat, lax.rem(lon + d, NZ))
+
+    def row_peer(d):
+        return ((lat & 6) | ((lat ^ d) & 25), lon)
+
+    def column_peer(d):
+        return ((lat & 25) | ((lat + 2 * d) & 6), lon)
+
     barrier = pltpu.get_barrier_semaphore()
-    for d in (8, 7, 9, 6, 10, 5, 11, 4, 12, 3, 13, 2, 14, 1, 15):
-        pl.semaphore_signal(
-            barrier, inc=1, device_id=(lat, lax.rem(lon + d, NZ)), device_id_type=MESH
-        )
-
-    def greet(d, carry):
-        pl.semaphore_signal(
-            barrier, inc=1, device_id=(lax.rem(lat + d, NL), lon), device_id_type=MESH
-        )
-        return carry
-
-    lax.fori_loop(1, NL, greet, 0)
+    near = (4, 12, 3, 13, 2, 14, 1, 15)
+    far = (8, 7, 9, 6, 10, 5, 11)
+    greeted = [ring_peer(d) for d in near]
+    greeted += [row_peer(d) for d in (25, 24, 17, 16, 9, 8, 1)]
+    greeted += [column_peer(d) for d in (2, 1, 3)]
+    for peer in greeted:
+        pl.semaphore_signal(barrier, inc=1, device_id=peer, device_id_type=MESH)
     loads = [
         pltpu.make_async_copy(cot_hbm, grid.at[0], load_sem.at[0]),
         pltpu.make_async_copy(in_hbm, grid.at[1], load_sem.at[1]),
@@ -109,10 +113,8 @@
     ]
     for load in loads:
         load.start()
-    def send_lon(phase, p):
-        def step(s, carry):
-            half = lax.div(s + 1, 2)
-            d = jnp.where(lax.rem(s, 2) == 0, 8 + half, 8 - half)
+    def send_lon(phase, p, distances=far + near, own=True):
+        for d in distances:
             to = lax.rem(lon + d, NZ)
             pltpu.make_async_remote_copy(
                 src_ref=zs[p].at[phase, to],
@@ -122,10 +124,8 @@
                 device_id=(lat, to),
                 device_id_type=MESH,
             ).start()
-            return carry
-
-        lax.fori_loop(0, NZ - 1, step, 0)
-        zr[p][phase, lon] = zs[p][phase, lon]
+        if own:
+            zr[p][phase, lon] = zs[p][phase, lon]
 
     def wait_lon(phase, p, sem):
         some = zr[p].at[phase, pl.ds(0, NZ - 1)]
@@ -350,9 +350,15 @@
 
     loads[0].wait()
     pack(0, 0)
-    pl.semaphore_wait(barrier, NZ - 1 + NL - 1)
-    send_lon(0, 0)
     pack(0, 1)
+    pl.semaphore_wait(barrier, len(greeted))
+    for d in (4, 12):
+        pl.semaphore_signal(far_sem, inc=1, device_id=ring_peer(d), device_id_type=MESH)
+    for d in (2, 1, 3):
+        pl.semaphore_signal(col_sem, inc=1, device_id=column_peer(d), device_id_type=MESH)
+    send_lon(0, 0, near[::-1], False)
+    pl.semaphore_wait(far_sem, 2)
+    send_lon(0, 0, far)
     send_lon(0, 1)
     loads[1].wait()
     pack(1, 0)
@@ -415,6 +421,7 @@
         lax.fori_loop(0, M, one, 0, unroll=4)
 
     acc[...] = jnp.zeros_like(acc)
+    pl.semaphore_wait(col_sem, 3)
     analyse_lon(0, 0)
     analyse_lat(0, 0)
     analyse_lon(0, 1)
@@ -524,6 +531,8 @@
             pltpu.SemaphoreType.DMA((3, 2)),
             pltpu.SemaphoreType.DMA,
             pltpu.SemaphoreType.DMA,
+            pltpu.SemaphoreType.REGULAR,
+            pltpu.SemaphoreType.REGULAR,
         ],
         compiler_params=pltpu.CompilerParams(
             collective_id=0, has_side_effects=True, vmem_limit_bytes=56 * 1024 * 1024

time: 81 us -> 78.3 us (0.967)
  Pallas kernels: 80.2 us -> 77.5 us
    pallas_call x1, Pallas kernels: 78.4 us -> 75.6 us  [local(): pl.pallas_call(kernel, out_shape=(jax.ShapeDtypeStruct((Q, N, CHANNELS),...]
where the time goes in v3:
time: 78.3 us; the launch traced here: 78.1 us
  Pallas kernels  77.5 us (99%)
    pallas_call x1, Pallas kernels, local(): pl.pallas_call(kernel, out_shape=(jax.ShapeDtypeStruct((Q, N, CHANNELS),...  75.6 us
    pallas_call x1, Pallas kernels, local(): pl.pallas_call(hand_over, out_shape=tuple((jax.ShapeDtypeStruct(out.shape...  1.82 us

profile of v3, /device:TPU:1, one launch (start us, length us, event | category | flops | bytes accessed | tf_op | source)
XLA Modules:
  0.0 78.1 jit_solution(12889517332411032971)
XLA Ops:
  0.6 75.6 %shard_map.77 = (bf16[12,48,384]{2,1,0:T(8,128)(2,1)}, f32[12,2,24]{2,1,0:T(2,128)}) custom-call(bf16[12,48,384]{2,1,0:T(8,128)(2,1)} %in_hbm.1, bf16[12,48,384]{2,1,0:T(8,128)(2,1)} %cot_hbm.1, bf16[12,384,384]{2,1,0:T(8,128)(2,1)} %leg_hbm.1, f32[2,24,384]{2,1,0:T(8,128)} %bitcast.1, bf16[768,768]{1,0:T(8,128)(2,1)} %constant.4.clone.fwd_hbm, ...), custom_call_target="tpu_custom_call" | custom-call | tf_op jit(solution)/shard_map/pallas_call | solution.py:489
  76.3 1.8 %shard_map.78 = (bf16[12,48,384]{2,1,0:T(8,128)(2,1)}, f32[12,2,24]{2,1,0:T(2,128)}) custom-call(bf16[12,48,384]{2,1,0:T(8,128)(2,1)} %get-tuple-element.4.grad_in, f32[12,2,24]{2,1,0:T(2,128)} %get-tuple-element.5.filt_in), custom_call_target="tpu_custom_call" | custom-call | tf_op jit(solution)/shard_map/pallas_call | solution.py:543

commit v4 on v3

--- a/solution.py
+++ b/solution.py
@@ -468,18 +468,14 @@
             first, count = PARTS[p]
             low = 2 * SLOT * p + SLOT * r
             filt_out[:, r, first : first + count] = total[:, low : low + count]
-    unpack(1)
-
     for phase in range(3):
         for p in range(2):
-            wait_lon(phase, p, zss)
+            if (phase, p) != (2, 1):
+                wait_lon(phase, p, zss)
             wait_lat(phase, p, lss)
     pltpu.make_async_copy(some, some, gss).wait()
-
-
-def hand_over(grad_in, filt_in, grad_out, filt_out):
-    grad_out[...] = grad_in[...]
-    filt_out[...] = filt_in[...]
+    unpack(1)
+    wait_lon(2, 1, zss)
 
 
 def local(grid_in, grid_cot, legendre, filters):
@@ -488,10 +484,7 @@
     any_space = pl.BlockSpec(memory_space=pl.ANY)
     outs = pl.pallas_call(
         kernel,
-        out_shape=(
-            jax.ShapeDtypeStruct((Q, N, CHANNELS), BF16),
-            jax.ShapeDtypeStruct((Q, 2, C), F32),
-        ),
+        out_shape=(vmem((Q, N, CHANNELS), BF16), vmem((Q, 2, C), F32)),
         in_specs=[any_space] * 6,
         out_specs=(pl.BlockSpec(memory_space=vmem), pl.BlockSpec(memory_space=vmem)),
         scratch_shapes=[
@@ -540,12 +533,7 @@
     )(
         grid_in, grid_cot, legendre, jnp.transpose(filters, (1, 2, 0)), jnp.asarray(fwd), jnp.asarray(bwd)
     )
-    return pl.pallas_call(
-        hand_over,
-        out_shape=tuple(jax.ShapeDtypeStruct(out.shape, out.dtype) for out in outs),
-        in_specs=[pl.BlockSpec(memory_space=vmem)] * 2,
-        out_specs=(pl.BlockSpec(memory_space=vmem), pl.BlockSpec(memory_space=vmem)),
-    )(*outs)
+    return outs
 
 
 def solution(mesh):

time: 78.3 us -> 77 us (0.983)
  Pallas kernels: 77.5 us -> 74.9 us
  local copies, waits for them, and re-layouts: 0 us -> 1.36 us
    pallas_call x2 -> x1, Pallas kernels: 77.5 us -> 74.9 us  [local(): pl.pallas_call(kernel, out_shape=(vmem((Q, N, CHANNELS), BF16), vmem((Q,...]
    unnamed x0 -> x2, local copies, waits for them, and re-layouts: none -> 1.36 us
where the time goes in v4:
time: 77 us; the launch traced here: 76.9 us
  Pallas kernels  74.9 us (97%)
  local copies, waits for them, and re-layouts  1.36 us (2%)
    pallas_call x1, Pallas kernels, local(): pl.pallas_call(kernel, out_shape=(vmem((Q, N, CHANNELS), BF16), vmem((Q,...  74.9 us

profile of v4, /device:TPU:1, one launch (start us, length us, event | category | flops | bytes accessed | tf_op | source)
XLA Modules:
  0.0 76.9 jit_solution(11587171441381877815)
XLA Ops:
  0.6 74.9 %shard_map.77 = (bf16[12,48,384]{2,1,0:T(8,128)(2,1)S(1)}, f32[12,2,24]{2,1,0:T(2,128)S(1)}) custom-call(bf16[12,48,384]{2,1,0:T(8,128)(2,1)} %in_hbm.1, bf16[12,48,384]{2,1,0:T(8,128)(2,1)} %cot_hbm.1, bf16[12,384,384]{2,1,0:T(8,128)(2,1)} %leg_hbm.1, f32[2,24,384]{2,1,0:T(8,128)} %bitcast.1, bf16[768,768]{1,0:T(8,128)(2,1)} %constant.4.clone.fwd_hbm, ...), custom_call_target="tpu_custom_call" | custom-call | tf_op jit(solution)/shard_map/pallas_call | solution.py:485
  75.5 0.8 copy.10
  76.3 0.6 copy.11

commit v5 on v4

--- a/solution.py
+++ b/solution.py
@@ -476,6 +476,17 @@
     pltpu.make_async_copy(some, some, gss).wait()
     unpack(1)
     wait_lon(2, 1, zss)
+
+
+def hand_over(grad_in, filt_in, grad_out, filt_out, sem):
+    copies = [
+        pltpu.make_async_copy(grad_in, grad_out, sem.at[0]),
+        pltpu.make_async_copy(filt_in, filt_out, sem.at[1]),
+    ]
+    for copy in copies:
+        copy.start()
+    for copy in copies:
+        copy.wait()
 
 
 def local(grid_in, grid_cot, legendre, filters):
@@ -533,7 +544,17 @@
     )(
         grid_in, grid_cot, legendre, jnp.transpose(filters, (1, 2, 0)), jnp.asarray(fwd), jnp.asarray(bwd)
     )
-    return outs
+    held = [pltpu.with_memory_space_constraint(out, pltpu.VMEM) for out in outs]
+    return pl.pallas_call(
+        hand_over,
+        out_shape=(
+            jax.ShapeDtypeStruct((Q, N, CHANNELS), BF16),
+            jax.ShapeDtypeStruct((Q, 2, C), F32),
+        ),
+        in_specs=[pl.BlockSpec(memory_space=vmem)] * 2,
+        out_specs=(any_space, any_space),
+        scratch_shapes=[pltpu.SemaphoreType.DMA((2,))],
+    )(*held)
 
 
 def solution(mesh):

time: 77 us -> 76.6 us (level)
  local copies, waits for them, and re-layouts: 1.36 us -> 0 us
  Pallas kernels: 74.9 us -> 75.7 us
    unnamed x2 -> x0, local copies, waits for them, and re-layouts: 1.36 us -> none
    pallas_call x0 -> x1, Pallas kernels: none -> 0.78 us  [local(): pl.pallas_call(hand_over, out_shape=(jax.ShapeDtypeStruct((Q, N, CHANNELS...]
where the time goes in v5:
time: 76.6 us; the launch traced here: 76.5 us
  Pallas kernels  75.7 us (99%)
  between operations  0.8 us (1%)
    pallas_call x1, Pallas kernels, local(): pl.pallas_call(kernel, out_shape=(vmem((Q, N, CHANNELS), BF16), vmem((Q,...  74.9 us

profile of v5, /device:TPU:1, one launch (start us, length us, event | category | flops | bytes accessed | tf_op | source)
XLA Modules:
  0.0 76.5 jit_solution(8665279526165010272)
XLA Ops:
  0.6 74.9 %shard_map.77 = (bf16[12,48,384]{2,1,0:T(8,128)(2,1)S(1)}, f32[12,2,24]{2,1,0:T(2,128)S(1)}) custom-call(bf16[12,48,384]{2,1,0:T(8,128)(2,1)} %in_hbm.1, bf16[12,48,384]{2,1,0:T(8,128)(2,1)} %cot_hbm.1, bf16[12,384,384]{2,1,0:T(8,128)(2,1)} %leg_hbm.1, f32[2,24,384]{2,1,0:T(8,128)} %bitcast.1, bf16[768,768]{1,0:T(8,128)(2,1)} %constant.4.clone.fwd_hbm, ...), custom_call_target="tpu_custom_call" | custom-call | tf_op jit(solution)/shard_map/pallas_call | solution.py:496
  75.5 0.8 %shard_map.78 = (bf16[12,48,384]{2,1,0:T(8,128)(2,1)}, f32[12,2,24]{2,1,0:T(2,128)}) custom-call(bf16[12,48,384]{2,1,0:T(8,128)(2,1)S(1)} %get-tuple-element.4.grad_in, f32[12,2,24]{2,1,0:T(2,128)S(1)} %get-tuple-element.5.filt_in), custom_call_target="tpu_custom_call" | custom-call | tf_op jit(solution)/shard_map/pallas_call | solution.py:548

commit v6 on v5

--- a/solution.py
+++ b/solution.py
@@ -66,6 +66,22 @@
     return pltpu.roll(wide, (size - shift) % size, 1) if shift % size else wide
 
 
+def grid_row(pbuf, p, q):
+    first, count = PARTS[p]
+    at = lanes(N)
+    start = first + count * q
+    tiles = []
+    for t in range(3):
+        low = 128 * t - start
+        z = low // C
+        value = pbuf[z % NZ, :, 128 * t : 128 * (t + 1)]
+        while C * (z + 1) - low < 128:
+            z += 1
+            value = jnp.where(at >= C * z - low, pbuf[z % NZ, :, 128 * t : 128 * (t + 1)], value)
+        tiles.append(value)
+    return shift_left(tiles, count * q)
+
+
 def one_hot(size, column_of):
     row = lax.broadcasted_iota(jnp.int32, (size, size), 0)
     column = lax.broadcasted_iota(jnp.int32, (size, size), 1)
@@ -78,8 +94,8 @@
 
 def kernel(
     in_hbm, cot_hbm, leg_hbm, filt_hbm, fwd_hbm, bwd_hbm,
-    grad_out, filt_out,
-    grid, leg, legp, filt, fwd, bwd, perm, permt, ring, pbuf, gain, xbuf, dbuf, xform, strans, sback, coef, acc,
+    grad_out, filt_out, pbuf,
+    grid, leg, legp, filt, fwd, bwd, perm, permt, ring, gain, xbuf, dbuf, xform, strans, sback, coef, acc,
     zs_a, zs_b, zr_a, zr_b, ls_a, ls_b, lr_a, lr_b, gs, gr,
     load_sem, own_sem, zss, zrs, lss, lrs, gss, grs, far_sem, col_sem,
 ):
@@ -325,28 +341,9 @@
                 turn = (C * z + first - shift) % RING
                 wide = jnp.concatenate(window, axis=1)
                 pbuf[z, 16 * g : 16 * (g + 1), :] = pltpu.roll(wide, turn, 1) if turn else wide
-        at = lanes(N)
-        for q in range(Q):
-            start = first + count * q
-            tiles = []
-            for t in range(3):
-                low = 128 * t - start
-                z = low // C
-                value = pbuf[z % NZ, :, 128 * t : 128 * (t + 1)]
-                while C * (z + 1) - low < 128:
-                    z += 1
-                    value = jnp.where(
-                        at >= C * z - low, pbuf[z % NZ, :, 128 * t : 128 * (t + 1)], value
-                    )
-                tiles.append(value)
-            whole = shift_left(tiles, count * q)
-            if p == 0:
-                grad_out[q] = whole
-            else:
-                for t in range(3):
-                    span = slice(128 * t, 128 * (t + 1))
-                    inner = lax.rem(at + 128 * t, C)
-                    grad_out[q, :, span] = jnp.where(inner < first, grad_out[q, :, span], whole[:, span])
+        if p == 0:
+            for q in range(Q):
+                grad_out[q] = grid_row(pbuf, p, q)
 
     loads[0].wait()
     pack(0, 0)
@@ -478,13 +475,20 @@
     wait_lon(2, 1, zss)
 
 
-def hand_over(grad_in, filt_in, grad_out, filt_out, sem):
-    copies = [
-        pltpu.make_async_copy(grad_in, grad_out, sem.at[0]),
-        pltpu.make_async_copy(filt_in, filt_out, sem.at[1]),
-    ]
-    for copy in copies:
+def hand_over(grad_in, filt_in, pbuf, grad_out, filt_out, row, sem):
+    first = PARTS[1][0]
+    at = lanes(N)
+    copies = [pltpu.make_async_copy(filt_in, filt_out, sem.at[Q])]
+    copies[0].start()
+    for q in range(Q):
+        whole = grid_row(pbuf, 1, q)
+        for t in range(3):
+            span = slice(128 * t, 128 * (t + 1))
+            inner = lax.rem(at + 128 * t, C)
+            row[q, :, span] = jnp.where(inner < first, grad_in[q, :, span], whole[:, span])
+        copy = pltpu.make_async_copy(row.at[q], grad_out.at[q], sem.at[q])
         copy.start()
+        copies.append(copy)
     for copy in copies:
         copy.wait()
 
@@ -495,9 +499,9 @@
     any_space = pl.BlockSpec(memory_space=pl.ANY)
     outs = pl.pallas_call(
         kernel,
-        out_shape=(vmem((Q, N, CHANNELS), BF16), vmem((Q, 2, C), F32)),
+        out_shape=(vmem((Q, N, CHANNELS), BF16), vmem((Q, 2, C), F32), vmem((NZ, N, RING), BF16)),
         in_specs=[any_space] * 6,
-        out_specs=(pl.BlockSpec(memory_space=vmem), pl.BlockSpec(memory_space=vmem)),
+        out_specs=(pl.BlockSpec(memory_space=vmem),) * 3,
         scratch_shapes=[
             vmem((2, Q, N, CHANNELS), BF16),
             vmem((M, LATS, DEGREES), BF16),
@@ -508,7 +512,6 @@
             vmem((512, 512), BF16),
             vmem((512, 512), BF16),
             vmem((K, NL, 512), F32),
-            vmem((NZ, N, RING), BF16),
             vmem((2, 2, SLOT, DEGREES), F32),
             vmem((768, 256), BF16),
             vmem((768, 256), F32),
@@ -551,9 +554,9 @@
             jax.ShapeDtypeStruct((Q, N, CHANNELS), BF16),
             jax.ShapeDtypeStruct((Q, 2, C), F32),
         ),
-        in_specs=[pl.BlockSpec(memory_space=vmem)] * 2,
+        in_specs=[pl.BlockSpec(memory_space=vmem)] * 3,
         out_specs=(any_space, any_space),
-        scratch_shapes=[pltpu.SemaphoreType.DMA((2,))],
+        scratch_shapes=[vmem((Q, N, CHANNELS), BF16), pltpu.SemaphoreType.DMA((Q + 1,))],
     )(*held)
 
 

time: 76.6 us -> 76.6 us (level)
  no operation moved by 1% of the time
where the time goes in v6:
time: 76.6 us; the launch traced here: 76.5 us
  Pallas kernels  75.7 us (99%)
  between operations  0.8 us (1%)
    pallas_call x1, Pallas kernels, local(): pl.pallas_call(kernel, out_shape=(vmem((Q, N, CHANNELS), BF16), vmem((Q,...  74.5 us

profile of v6, /device:TPU:1, one launch (start us, length us, event | category | flops | bytes accessed | tf_op | source)
XLA Modules:
  0.0 76.5 jit_solution(2172812755202288035)
XLA Ops:
  0.6 74.5 %shard_map.77 = (bf16[12,48,384]{2,1,0:T(8,128)(2,1)S(1)}, f32[12,2,24]{2,1,0:T(2,128)S(1)}, bf16[16,48,384]{2,1,0:T(8,128)(2,1)S(1)}) custom-call(bf16[12,48,384]{2,1,0:T(8,128)(2,1)} %in_hbm.1, bf16[12,48,384]{2,1,0:T(8,128)(2,1)} %cot_hbm.1, bf16[12,384,384]{2,1,0:T(8,128)(2,1)} %leg_hbm.1, f32[2,24,384]{2,1,0:T(8,128)} %bitcast.1, ...), custom_call_target="tpu_custom_call" | custom-call | tf_op jit(solution)/shard_map/pallas_call | solution.py:500
  75.2 1.1 %shard_map.78 = (bf16[12,48,384]{2,1,0:T(8,128)(2,1)}, f32[12,2,24]{2,1,0:T(2,128)}) custom-call(bf16[12,48,384]{2,1,0:T(8,128)(2,1)S(1)} %get-tuple-element.5.grad_in, f32[12,2,24]{2,1,0:T(2,128)S(1)} %get-tuple-element.6.filt_in, bf16[16,48,384]{2,1,0:T(8,128)(2,1)S(1)} %get-tuple-element.7.pbuf), custom_call_target="tpu_custom_call" | custom-call | tf_op jit(solution)/shard_map/pallas_call | solution.py:551
